TPU v7x, 256 devices: a whole 4x4x8 slice. The times are simulated.
256 devices in a mesh: grp: 16 (over y, x), sub: 16 (over z, core).
Axes of the slice: x: 4, y: 4, z: 8, core: 2. Of those that a mesh axis runs over, the one named last changes fastest.
Arguments:
- loads: bfloat16 [512, 1024, 128], P(('grp', 'sub')), may hold values from -6 to 6
- schur: bfloat16 [512, 1024, 1024], P(('grp', 'sub')), may hold values from -0.5 to 3.5, as said below
- neumann: bfloat16 [512, 1024, 1024], P(('grp', 'sub')), may hold values from -0.5 to 1.5, as said below
- basis: bfloat16 [512, 24, 1024], P(('grp', 'sub')), may hold values from -0.375 to 0.375
- dof_order: int32 [512, 4, 256], P(('grp', 'sub')), may hold values from 0 to 255, each once within a row
- primal_map: int32 [512, 24], P(('grp', 'sub')), may hold values from 0 to 2047
- emitter_counts: int32 [512], replicated, may hold values from 0 to 15
- coarse_inverse: float32 [2048, 2048], P('sub'), may hold values from -0.5 to 0.5, as said below
Outputs:
- solution: float32 [512, 1024, 128], P(('grp', 'sub'))
Inputs may be any that keep to these rules, and one draw needn't show every extreme that they name: `schur`: each block is symmetric positive definite. `neumann`: each block is symmetric positive definite. `coarse_inverse`: symmetric positive definite.
All inputs are finite; a program needn't handle non-finite values.
Results may differ from a plain program's by a relative error of at most 0.0022.
Values sent between devices are 32-bit elements; how exact they have to be, the bound alone decides.
No kernel may reach another device: no remote copies, remote signals or barrier semaphores. Data moves between devices by JAX's collectives and lax.ppermute only.
A program may use at most 64 MiB of HBM per device.

v0:
```python
import jax
import jax.numpy as jnp
from jax import lax
from jax.sharding import PartitionSpec as P

ITERS = 2


HIGHEST = lax.Precision.HIGHEST


def with_halo(value, sides, width):
    for axis, dim in sides:
        peers, length = (lax.axis_size(axis), value.shape[dim])
        up = [(i, (i + 1) % peers) for i in range(peers - 1)]
        down = [(j, i) for i, j in up]
        last = lax.slice_in_dim(value, length - width, length, axis=dim)
        leading = lax.slice_in_dim(value, 0, width, axis=dim)
        before = lax.ppermute(last, axis, up)
        after = lax.ppermute(leading, axis, down)
        value = jnp.concatenate([before, value, after], axis=dim)
    return value


def body(loads, schur, neumann, basis, dof_order, primal_map, emitter_counts, coarse_inverse):
    sub_dev, width, columns = loads.shape
    face = width // 4
    n_grp = lax.axis_size("grp")
    n_sub = lax.axis_size("sub")
    grp_index = lax.axis_index("grp")
    sub_index = lax.axis_index("sub")
    chain = n_sub * sub_dev
    coarse_count = coarse_inverse.shape[1]
    row_index = (jnp.arange(4, dtype=jnp.int32)[None, :, None] * face + dof_order).reshape(
        sub_dev, width
    )
    inverse = jnp.argsort(row_index, axis=1)
    density = 1.0 + emitter_counts.astype(jnp.float32).reshape(n_grp, chain)
    padded = jnp.pad(density, 1)
    start_col = sub_index * sub_dev

    def window(row_start, col_start):
        return lax.dynamic_slice(padded, (row_start, col_start), (1, sub_dev))[0]

    own_rho = window(grp_index + 1, start_col + 1)[:, None]
    beside = jnp.stack(
        [
            window(grp_index, start_col + 1),
            window(grp_index + 2, start_col + 1),
            window(grp_index + 1, start_col),
            window(grp_index + 1, start_col + 2),
        ],
        axis=1,
    )
    weights = jnp.where(beside > 0.0, own_rho / (own_rho + beside), 1.0)
    share = jnp.repeat(weights, face, axis=1)[:, :, None]
    basis_wide = basis.astype(jnp.float32)

    def assemble(values):
        canon = jnp.take_along_axis(values, row_index[:, :, None], axis=1).reshape(
            sub_dev, 4, face, columns
        )
        slab_pair = jnp.stack([canon[:, 0], canon[:, 1]], axis=0)
        slab_wide = with_halo(slab_pair, (("grp", 0),), 1)
        column_pair = jnp.stack([canon[:, 2], canon[:, 3]], axis=1).reshape(
            sub_dev * 2, face, columns
        )
        column_wide = with_halo(column_pair, (("sub", 0),), 1)
        previous = column_wide[0 : 2 * sub_dev : 2]
        following = column_wide[3 : 2 * sub_dev + 2 : 2]
        partners = jnp.stack([slab_wide[0], slab_wide[3], previous, following], axis=1).reshape(
            sub_dev, width, columns
        )
        return values + jnp.take_along_axis(partners, inverse[:, :, None], axis=1)

    def local_inner(left, right):
        return jnp.sum(share * left * right, axis=(0, 1))

    selector = (
        primal_map[:, :, None] == jnp.arange(coarse_count, dtype=jnp.int32)[None, None, :]
    ).astype(jnp.float32)

    def precondition(residual):
        scaled = share * residual
        rounded = scaled.astype(jnp.bfloat16)
        local = jnp.einsum("sij,sjr->sir", neumann, rounded, preferred_element_type=jnp.float32)
        moments = jnp.einsum("spj,sjr->spr", basis, rounded, preferred_element_type=jnp.float32)
        partial_rhs = jnp.einsum("spc,spr->cr", selector, moments, precision=HIGHEST)
        gathered = lax.psum(partial_rhs, ("grp", "sub"))
        coarse_slab = jnp.dot(coarse_inverse, gathered, precision=HIGHEST)
        coarse = lax.all_gather(coarse_slab, "sub", axis=0, tiled=True)
        picked = jnp.take(coarse, primal_map, axis=0)
        local = local + jnp.einsum("spi,spr->sir", basis_wide, picked, precision=HIGHEST)
        search = assemble(share * local)
        inner_value = lax.psum(local_inner(residual, search), ("grp", "sub"))
        return (search, inner_value)

    residual = assemble(loads.astype(jnp.float32))
    solution = jnp.zeros((sub_dev, width, columns), jnp.float32)
    search, inner_now = precondition(residual)
    direction = search
    for iteration in range(ITERS):
        image = assemble(
            jnp.einsum(
                "sij,sjr->sir",
                schur,
                direction.astype(jnp.bfloat16),
                preferred_element_type=jnp.float32,
            )
        )
        curve = lax.psum(local_inner(direction, image), ("grp", "sub"))
        step_size = inner_now / curve
        solution = solution + step_size * direction
        residual = residual - step_size * image
        if iteration + 1 < ITERS:
            search, inner_next = precondition(residual)
            direction = search + inner_next / inner_now * direction
            inner_now = inner_next
    return solution


def solution(mesh):
    in_specs = (
        P(("grp", "sub"), None, None),
        P(("grp", "sub"), None, None),
        P(("grp", "sub"), None, None),
        P(("grp", "sub"), None, None),
        P(("grp", "sub"), None, None),
        P(("grp", "sub"), None),
        P(),
        P("sub", None),
    )
    out_specs = P(("grp", "sub"), None, None)
    return jax.shard_map(body, mesh=mesh, in_specs=in_specs, out_specs=out_specs, check_vma=False)
```

profile of v0, /device:TPU:1, one launch (start us, length us, event | category | flops | bytes accessed | tf_op | source)
XLA Modules:
  0.0 1222.3 jit_solution(700045894645351845)
XLA Ops:
  8.9 22.7 %gather_fusion = f32[2048,128]{1,0:T(8,128)} fusion(f32[2,1024,128]{2,1,0:T(8,128)S(1)} %copy.36, s32[2048]{0:T(1024)S(1)} %bitcast.189), kind=kCustom, calls=%fused_computation.clone | custom fusion | bytes 2113536 | tf_op jit(solution)/shard_map/jit(take_along_axis)/gather | solution.py:60
  34.0 4.9 collective-permute-start.2
  47.1 4.5 sort.19.cloned.1.call-done
  53.2 22.7 %gather_fusion.1 = f32[2048,128]{1,0:T(8,128)} fusion(f32[2,1024,128]{2,1,0:T(8,128)S(1)} %bitcast.200, s32[2048]{0:T(1024)S(1)} %bitcast.194), kind=kCustom, calls=%fused_computation.2.clone | custom fusion | bytes 2113536 | tf_op jit(solution)/shard_map/jit(take_along_axis)/gather | solution.py:74
  80.3 259.6 %all-reduce.5.cloned.1.call-done = f32[2048,128]{1,0:T(8,128)} async-done(((f32[2048,128]{1,0:T(8,128)}), f32[2048,128]{1,0:T(8,128)}) %all-reduce.5.cloned.1.call-update) | async-done | bytes 1048592 | tf_op jit(solution)/shard_map/psum | solution.py:89
  343.8 4.7 fusion.34
  348.5 33.5 %all-gather.3.cloned.1.call-done = f32[2048,128]{0,1:T(8,128)} async-done(((f32[128,128]{0,1:T(8,128)}), f32[2048,128]{0,1:T(8,128)}) %all-gather.3.cloned.1.call-update) | async-done | bytes 1048592 | tf_op jit(solution)/shard_map/all_gather | solution.py:91
  386.4 22.7 %gather_fusion.3 = f32[2048,128]{1,0:T(8,128)} fusion(f32[2,1024,128]{2,1,0:T(8,128)S(1)} %copy.42, s32[2048]{0:T(1024)S(1)} %bitcast.190), kind=kCustom, calls=%fused_computation.3.clone | custom fusion | bytes 2113536 | tf_op jit(solution)/shard_map/jit(take_along_axis)/gather | solution.py:60
  428.3 22.7 %gather_fusion.4 = f32[2048,128]{1,0:T(8,128)} fusion(f32[2,1024,128]{2,1,0:T(8,128)S(1)} %bitcast.201, s32[2048]{0:T(1024)S(1)} %bitcast.195), kind=kCustom, calls=%fused_computation.4.clone | custom fusion | bytes 2113536 | tf_op jit(solution)/shard_map/jit(take_along_axis)/gather | solution.py:74
  455.0 4.7 convolution_bitcast_fusion.3
  461.2 22.5 %gather_fusion.5 = f32[2048,128]{1,0:T(8,128)} fusion(f32[2,1024,128]{2,1,0:T(8,128)S(1)} %copy.47, s32[2048]{0:T(1024)S(1)} %bitcast.191), kind=kCustom, calls=%fused_computation.5.clone | custom fusion | bytes 2113536 | tf_op jit(solution)/shard_map/jit(take_along_axis)/gather | solution.py:60
  498.8 4.1 collective-permute-done.9
  503.0 22.5 %gather_fusion.6 = f32[2048,128]{1,0:T(8,128)} fusion(f32[2,1024,128]{2,1,0:T(8,128)S(1)} %bitcast.202, s32[2048]{0:T(1024)S(1)} %bitcast.196), kind=kCustom, calls=%fused_computation.6.clone | custom fusion | bytes 2113536 | tf_op jit(solution)/shard_map/jit(take_along_axis)/gather | solution.py:74
  530.5 79.2 %all-reduce.1 = (f32[128]{0:T(128)S(1)}, f32[128]{0:T(128)S(1)}) all-reduce(f32[128]{0:T(128)S(1)} %get-tuple-element.10, f32[128]{0:T(128)S(1)} %get-tuple-element.9), channel_id=1, replica_groups=mesh['grp'=16,'sub'=16] {'grp','sub'}, use_global_device_ids=true, to_apply=%region_3.6 | all-reduce | flops 256 | bytes 2048 | tf_op jit(solution)/shard_map/psum | solution.py:95
  615.5 249.9 %all-reduce.7.cloned.1.call-done = f32[2048,128]{1,0:T(8,128)} async-done(((f32[2048,128]{1,0:T(8,128)}), f32[2048,128]{1,0:T(8,128)}) %all-reduce.7.cloned.1.call-update) | async-done | bytes 1048592 | tf_op jit(solution)/shard_map/psum | solution.py:89
  869.1 4.7 fusion.12
  873.8 33.7 %all-gather.5.cloned.1.call-done = f32[2048,128]{0,1:T(8,128)} async-done(((f32[128,128]{0,1:T(8,128)}), f32[2048,128]{0,1:T(8,128)}) %all-gather.5.cloned.1.call-update) | async-done | bytes 1048592 | tf_op jit(solution)/shard_map/all_gather | solution.py:91
  914.1 22.5 %gather_fusion.8 = f32[2048,128]{1,0:T(8,128)} fusion(f32[2,1024,128]{2,1,0:T(8,128)S(1)} %copy.53, s32[2048]{0:T(1024)S(1)} %bitcast.192), kind=kCustom, calls=%fused_computation.7.clone | custom fusion | bytes 2113536 | tf_op jit(solution)/shard_map/jit(take_along_axis)/gather | solution.py:60
  951.7 4.1 collective-permute-done.13
  955.8 22.5 %gather_fusion.9 = f32[2048,128]{1,0:T(8,128)} fusion(f32[2,1024,128]{2,1,0:T(8,128)S(1)} %bitcast.203, s32[2048]{0:T(1024)S(1)} %bitcast.197), kind=kCustom, calls=%fused_computation.8.clone | custom fusion | bytes 2113536 | tf_op jit(solution)/shard_map/jit(take_along_axis)/gather | solution.py:74
  983.0 77.1 %psum.46 = f32[128]{0:T(128)S(1)} all-reduce(f32[128]{0:T(128)S(1)} %multiply_reduce_fusion), channel_id=1, replica_groups=mesh['grp'=16,'sub'=16] {'grp','sub'}, use_global_device_ids=true, to_apply=%region_8.11 | all-reduce | flops 128 | bytes 1024 | tf_op jit(solution)/shard_map/psum | solution.py:95
  1066.8 22.5 %gather_fusion.10 = f32[2048,128]{1,0:T(8,128)} fusion(f32[2,1024,128]{2,1,0:T(8,128)S(1)} %copy.58, s32[2048]{0:T(1024)S(1)} %bitcast.193), kind=kCustom, calls=%fused_computation.9.clone | custom fusion | bytes 2113536 | tf_op jit(solution)/shard_map/jit(take_along_axis)/gather | solution.py:60
  1107.1 22.5 %gather_fusion.11 = f32[2048,128]{1,0:T(8,128)} fusion(f32[2,1024,128]{2,1,0:T(8,128)S(1)} %bitcast.199, s32[2048]{0:T(1024)S(1)} %bitcast.198), kind=kCustom, calls=%fused_computation.10.clone | custom fusion | bytes 2113536 | tf_op jit(solution)/shard_map/jit(take_along_axis)/gather | solution.py:74
  1134.4 77.6 %psum.47 = f32[128]{0:T(128)S(1)} all-reduce(f32[128]{0:T(128)S(1)} %fusion.5), channel_id=1, replica_groups=mesh['grp'=16,'sub'=16] {'grp','sub'}, use_global_device_ids=true, to_apply=%region_10.13 | all-reduce | flops 128 | bytes 1024 | tf_op jit(solution)/shard_map/psum | solution.py:111
  (169 shorter events, 140.5 us)
Async XLA Ops:
  34.0 19.1 %collective-permute-start.2 = (f32[1,256,128]{2,1,0:T(8,128)}, f32[1,256,128]{2,1,0:T(8,128)S(1)}, u32[]{:S(2)}, u32[]{:S(2)}) collective-permute-start(f32[1,256,128]{2,1,0:T(8,128)} %get-tuple-element.41), channel_id=1, source_target_pairs={{0,1},{1,2},{2,3},{3,4},{4,5},{5,6},{6,7},{7,8},{8,9},{9,10},{10,1... | collective-permute-start | bytes 393224 | tf_op jit(solution)/shard_map/ppermute | solution.py:19
  38.9 14.1 %collective-permute-start.3 = (f32[1,256,128]{2,1,0:T(8,128)}, f32[1,256,128]{2,1,0:T(8,128)S(1)}, u32[]{:S(2)}, u32[]{:S(2)}) collective-permute-start(f32[1,256,128]{2,1,0:T(8,128)} %get-tuple-element.42), channel_id=1, source_target_pairs={{1,0},{2,1},{3,2},{4,3},{5,4},{6,5},{7,6},{8,7},{9,8},{10,9},{11,1... | collective-permute-start | bytes 393224 | tf_op jit(solution)/shard_map/ppermute | solution.py:20
  40.9 12.3 %collective-permute-start = (f32[1,2,256,128]{3,2,1,0:T(8,128)S(1)}, f32[1,2,256,128]{3,2,1,0:T(8,128)S(1)}, u32[]{:S(2)}, u32[]{:S(2)}) collective-permute-start(f32[1,2,256,128]{3,2,1,0:T(8,128)S(1)} %get-tuple-element.21), channel_id=1, source_target_pairs={{0,16},{16,32},{32,48},{48,64},{64,80},{80,96},{96,112},{112,128},... | collective-permute-start | bytes 786440 | tf_op jit(solution)/shard_map/ppermute | solution.py:19
  44.0 9.2 collective-permute-start.1
  46.6 293.3 %all-reduce.5.cloned.1.call-start = ((), (), s32[]{:S(2)}) async-start(), calls=%async_computation | async-start | bytes 2097152 | tf_op jit(solution)/shard_map/psum | solution.py:89
  80.3 301.7 %all-gather.3.cloned.1.call-start = ((), (), s32[]{:S(2)}) async-start(), calls=%async_computation.1 | async-start | bytes 1114112 | tf_op jit(solution)/shard_map/all_gather | solution.py:91
  343.6 521.8 %all-reduce.7.cloned.1.call-start = ((), (), s32[]{:S(2)}) async-start(), calls=%async_computation.2 | async-start | bytes 2097152 | tf_op jit(solution)/shard_map/psum | solution.py:89
  410.7 9.5 collective-permute-start.6
  413.6 6.6 collective-permute-start.7
  415.6 8.5 collective-permute-start.4
  418.7 9.5 collective-permute-start.5
  485.3 10.4 collective-permute-start.10
  489.4 6.4 collective-permute-start.11
  491.3 7.4 collective-permute-start.8
  494.4 8.4 collective-permute-start.9
  615.3 292.2 %all-gather.5.cloned.1.call-start = ((), (), s32[]{:S(2)}) async-start(), calls=%async_computation.3 | async-start | bytes 1114112 | tf_op jit(solution)/shard_map/all_gather | solution.py:91
  938.2 9.3 collective-permute-start.14
  941.1 6.4 collective-permute-start.15
  943.1 8.5 collective-permute-start.12
  946.2 9.5 collective-permute-start.13
  1090.9 9.4 collective-permute-start.18
  1095.0 6.3 collective-permute-start.19
  1097.0 5.9 collective-permute-start.16
  1098.7 8.3 collective-permute-start.17
  (15 other events, 1260.0 us)
Sparse Core Ops, SparseCore 0:
  46.7 4.5 sort.21.cloned.1.call-done
  80.4 259.4 all-reduce.4
  343.7 38.2 all-gather.2
  615.4 249.9 all-reduce.6
  869.2 38.2 all-gather.4
  (1 shorter events, 0.0 us)
where the time goes:
time: 1220 us
  waiting for transfers between devices  606 us (50%)
  local copies, waits for them, and re-layouts  260 us (21%)
  blocking collectives  234 us (19%)
  starting transfers between devices  50 us (4%)
  matrix products  33.7 us (3%)
  other arithmetic  24.1 us (2%)
  between operations  13.9 us (1%)
    psum x2, waiting for transfers between devices, precondition(): gathered = lax.psum(partial_rhs, ('grp', 'sub'))  509 us
    psum x2, blocking collectives, precondition(): inner_value = lax.psum(local_inner(residual, search), ('grp', 'sub'))  156 us
    gather x10, local copies, waits for them, and re-layouts, assemble(): return values + jnp.take_along_axis(partners, inverse[:, :, None], axis=1)  125 us
    gather x5, local copies, waits for them, and re-layouts, assemble(): jnp.take_along_axis(values, row_index[:, :, None], axis=1)  113 us
    psum x1, blocking collectives, body(): curve = lax.psum(local_inner(direction, image), ('grp', 'sub'))  77.6 us
    all_gather x2, waiting for transfers between devices, precondition(): coarse = lax.all_gather(coarse_slab, 'sub', axis=0, tiled=True)  67.2 us
    ppermute x10, starting transfers between devices, with_halo(): before = lax.ppermute(last, axis, up)  33.1 us
  transfers between devices with their start and end apart: 24, of which 13 were waited for; matrix products, arithmetic and copies ran while one was open for 1% of the time, Pallas kernels for 0%

commit v1 on v0

v1 whole, which is shorter than its diff:
```python
import functools

import jax
import jax.numpy as jnp
from jax import lax
from jax.experimental import pallas as pl
from jax.experimental.pallas import tpu as pltpu
from jax.sharding import PartitionSpec as P

F32 = jnp.float32
BF16 = jnp.bfloat16
AXES = ("grp", "sub")
LANES = 128
TILE = 8
FACE = 256
HI = 16
COLS = 4
GATHER = HI * COLS + TILE
VMEM_LIMIT = 40 * 1024 * 1024

NN = (((1,), (0,)), ((), ()))
NT = (((1,), (1,)), ((), ()))
TN = (((0,), (0,)), ((), ()))


def dot(left, right, dims=NN):
    return lax.dot_general(left, right, dims, preferred_element_type=F32)


def split(value):
    high = value.astype(BF16)
    return high, (value - high.astype(F32)).astype(BF16)


def wide(value):
    return jnp.concatenate(split(value), axis=1)


def fold(value):
    return value[:, :LANES] + value[:, LANES:]


def to_canon(order, value):
    return fold(dot(order, wide(value), TN))


def to_local(order, value):
    return fold(dot(order, wide(value)))


def rows(face):
    return pl.ds(face * FACE, FACE)


def call(kernel, out_shapes, *args, smem=(), cost=None):
    specs = [
        pl.BlockSpec(memory_space=pltpu.SMEM if i in smem else pltpu.VMEM)
        for i in range(len(args))
    ]
    return pl.pallas_call(
        kernel,
        out_shape=[jax.ShapeDtypeStruct(s, d) for s, d in out_shapes],
        in_specs=specs,
        out_specs=[pl.BlockSpec(memory_space=pltpu.VMEM) for _ in out_shapes],
        compiler_params=pltpu.CompilerParams(vmem_limit_bytes=VMEM_LIMIT),
    )(*args)


HALO_SHAPES = [
    ((2, FACE, LANES), F32),
    ((2, FACE, LANES), F32),
    ((FACE, LANES), F32),
    ((FACE, LANES), F32),
    ((2, FACE, LANES), F32),
]


def put_faces(send, order_ref, value_of, one_pass=False):
    up, down, after, before, inside = send

    def canon(s, f):
        order = order_ref[4 * s + f]
        if one_pass:
            return dot(order, value_of(s, f), TN)
        return to_canon(order, value_of(s, f))

    for s in range(2):
        up[s] = canon(s, 1)
        down[s] = canon(s, 0)
    after[...] = canon(1, 3)
    before[...] = canon(0, 2)
    inside[0] = canon(0, 3)
    inside[1] = canon(1, 2)


def partner(recv, s, f):
    lower, upper, previous, following, inside = recv
    if f == 0:
        return lower[s]
    if f == 1:
        return upper[s]
    if f == 2:
        return previous[...] if s == 0 else inside[0]
    return inside[1] if s == 0 else following[...]


def exchange(send):
    up, down, after, before, inside = send
    n_grp = lax.axis_size("grp")
    n_sub = lax.axis_size("sub")
    grp_up = [(i, i + 1) for i in range(n_grp - 1)]
    grp_down = [(i + 1, i) for i in range(n_grp - 1)]
    sub_up = [(i, i + 1) for i in range(n_sub - 1)]
    sub_down = [(i + 1, i) for i in range(n_sub - 1)]
    lower = lax.ppermute(up, "grp", grp_up)
    upper = lax.ppermute(down, "grp", grp_down)
    previous = lax.ppermute(after, "sub", sub_up)
    following = lax.ppermute(before, "sub", sub_down)
    return [lower, upper, previous, following, inside]


def share_of(share_ref, s, f):
    return share_ref[pl.ds(4 * s + f, 1), :]


def prepare_kernel(place, counts, dof, loads, order, share, *send):
    grp, sub = place[0], place[1]
    n_grp, n_sub = place[2], place[3]
    chain = 2 * n_sub

    def density(g, j):
        inside = (g >= 0) & (g < n_grp) & (j >= 0) & (j < chain)
        at = jnp.where(inside, g * chain + j, 0)
        return jnp.where(inside, counts[at].astype(F32) + 1.0, 0.0)

    for s in range(2):
        j = 2 * sub + s
        own = jnp.full((1, LANES), density(grp, j), F32)
        near = ((grp - 1, j), (grp + 1, j), (grp, j - 1), (grp, j + 1))
        for f, (g, k) in enumerate(near):
            beside = jnp.full((1, LANES), density(g, k), F32)
            share[pl.ds(4 * s + f, 1), :] = own / (own + beside)
    row = lax.broadcasted_iota(jnp.int32, (FACE, FACE), 0)
    for s in range(2):
        for f in range(4):
            order[4 * s + f] = (row == dof[s, pl.ds(f, 1), :]).astype(F32).astype(BF16)
    put_faces(send, order, lambda s, f: loads[s, rows(f), :], one_pass=True)


def coarse_split_kernel(place, own, other, high, low):
    core = place[1] % 2
    for half in range(2):
        at = pl.ds(half * LANES, LANES)
        value = jnp.where(core == half, own[...], other[...])
        first, second = split(value)
        high[at, :] = first
        low[at, :] = second


def put_message(message, values, index):
    flat = jnp.transpose(values)
    owners = LANES // COLS
    for c in range(COLS):
        message[pl.ds(c, owners, stride=TILE), :] = flat[c * owners : (c + 1) * owners]
    message[pl.ds(COLS, owners, stride=TILE), :] = jnp.broadcast_to(index[...], (owners, LANES))
    for c in range(COLS + 1, TILE):
        message[pl.ds(c, owners, stride=TILE), :] = jnp.zeros((owners, LANES), F32)


def get_message(message):
    owners = LANES // COLS
    flat = jnp.concatenate(
        [message[pl.ds(c, owners, stride=TILE), :] for c in range(COLS)], axis=0
    )
    return jnp.transpose(flat)


def residual_kernel(
    loads, lower, upper, previous, following, inside, order, share, neumann, basis, index,
    residual, local, message,
):
    recv = (lower, upper, previous, following, inside)
    moments = []
    for s in range(2):
        pieces = []
        for f in range(4):
            beside = dot(order[4 * s + f], partner(recv, s, f).astype(BF16))
            value = loads[s, rows(f), :].astype(F32) + beside
            residual[s, rows(f), :] = value
            pieces.append((share_of(share, s, f) * value).astype(BF16))
        rounded = jnp.concatenate(pieces, axis=0)
        local[s] = dot(neumann[s], rounded)
        moments.append(dot(basis[s], rounded))
    used = sum(m.shape[0] for m in moments)
    moments.append(jnp.zeros((LANES - used, LANES), F32))
    put_message(message, jnp.concatenate(moments, axis=0), index)


def scatter_kernel(received, gathered, lhs, hot):
    owners = received.shape[0] // TILE
    row = lax.broadcasted_iota(jnp.int32, (LANES, LANES), 0)
    total = jnp.zeros((TILE, LANES), F32)
    for d in range(owners):
        block = received[pl.ds(TILE * d, TILE), :]
        total = total + block
        at = block[COLS : COLS + 1].astype(jnp.int32)
        high = at >> 7
        low = at & (LANES - 1)
        span = pl.ds(d * LANES, LANES)
        hot[:, span] = (row == low).astype(F32).astype(BF16)
        spread = jnp.concatenate(
            [jnp.where(high == h, block, 0.0) for h in range(HI)], axis=0
        )
        first, second = split(spread)
        lhs[pl.ds(0, LANES), span] = first
        lhs[pl.ds(LANES, LANES), span] = second
    both = dot(lhs[...], hot[...], NT)
    sums = both[:LANES] + both[LANES:]
    packed = [sums[TILE * h : TILE * h + COLS] for h in range(HI)]
    packed = jnp.concatenate(packed + [total], axis=0)
    for z in range(gathered.shape[0] // GATHER):
        gathered[pl.ds(GATHER * z, GATHER), :] = packed


def coarse_kernel(gathered, high, low, slab, scalars):
    n_z = gathered.shape[0] // GATHER
    total = gathered[pl.ds(0, GATHER), :]
    for z in range(1, n_z):
        total = total + gathered[pl.ds(GATHER * z, GATHER), :]
    scalars[...] = total[HI * COLS :]
    flat = jnp.concatenate([total[COLS * h : COLS * h + COLS] for h in range(HI)], axis=1)
    first, second = split(flat)
    both = dot(jnp.concatenate([first, second], axis=0), high[...], NT)
    result = both[:COLS] + both[COLS:] + dot(first, low[...], NT)
    tile = jnp.concatenate([result[:, :LANES], result[:, LANES:]], axis=0)
    for z in range(n_z):
        slab[pl.ds(TILE * z, TILE), :] = tile


def pick_kernel(coarse, received, scalars, message):
    owners = received.shape[0] // TILE
    row = lax.broadcasted_iota(jnp.int32, (LANES, LANES), 0)
    tile_row = lax.broadcasted_iota(jnp.int32, (TILE, LANES), 0)
    lane = lax.broadcasted_iota(jnp.int32, (TILE, LANES), 1)
    first, second = split(coarse[...])
    table = jnp.concatenate([first, second], axis=0)
    extra = scalars[...]
    for d in range(owners):
        at = received[pl.ds(TILE * d + COLS, 1), :].astype(jnp.int32)
        high = at >> 7
        low = at & (LANES - 1)
        hot = (row == low).astype(F32).astype(BF16)
        both = dot(table, hot)
        value = both[: HI * COLS] + both[HI * COLS :]
        total = jnp.zeros((TILE, LANES), F32)
        for v in range(HI * COLS // TILE):
            here = high == (tile_row // COLS + 2 * v)
            total = total + jnp.where(here, value[TILE * v : TILE * v + TILE], 0.0)
        total = total + pltpu.roll(total, COLS, 0)
        message[pl.ds(TILE * d, TILE), :] = jnp.where(lane < 48, total, extra)


def spread_basis(basis, s, picked):
    prim = basis.shape[1]
    here = picked[prim * s : prim * s + prim]
    first = here.astype(BF16).astype(F32)
    second = here - first
    both = jnp.concatenate([first, second], axis=0).astype(BF16)
    twice = jnp.concatenate([basis[s].astype(F32)] * 2, axis=0).astype(BF16)
    return dot(twice, both, TN)


def search_kernel(message, local, basis, share, order, partial, *send):
    picked = get_message(message)
    for s in range(2):
        value = local[s] + spread_basis(basis, s, picked)
        for f in range(4):
            part = value[f * FACE : f * FACE + FACE]
            partial[s, rows(f), :] = share_of(share, s, f) * part
    put_faces(send, order, lambda s, f: partial[s, rows(f), :])


def direction_kernel(
    partial, lower, upper, previous, following, inside, order, share, schur, residual,
    direction, image, scalars, *send,
):
    recv = (lower, upper, previous, following, inside)
    rz = jnp.zeros((1, LANES), F32)
    curve = jnp.zeros((1, LANES), F32)
    for s in range(2):
        for f in range(4):
            value = partial[s, rows(f), :] + to_local(order[4 * s + f], partner(recv, s, f))
            direction[s, rows(f), :] = value
            weighted = share_of(share, s, f) * residual[s, rows(f), :] * value
            rz = rz + jnp.sum(weighted, axis=0, keepdims=True)
        whole = direction[s]
        product = dot(schur[s], whole.astype(BF16))
        image[s] = product
        curve = curve + jnp.sum(whole * product, axis=0, keepdims=True)
    scalars[...] = jnp.concatenate([rz, curve, jnp.zeros((TILE - 2, LANES), F32)], axis=0)
    put_faces(send, order, lambda s, f: image[s, rows(f), :])


def image_kernel(
    partial, lower, upper, previous, following, inside, order, share, basis, index, scalars,
    image, message,
):
    recv = (lower, upper, previous, following, inside)
    moments = []
    for s in range(2):
        pieces = []
        for f in range(4):
            value = partial[s, rows(f), :] + to_local(order[4 * s + f], partner(recv, s, f))
            image[s, rows(f), :] = value
            pieces.append(wide(share_of(share, s, f) * value))
        moments.append(fold(dot(basis[s], jnp.concatenate(pieces, axis=0))))
    moments.append(scalars[...])
    used = sum(m.shape[0] for m in moments)
    moments.append(jnp.zeros((LANES - used, LANES), F32))
    put_message(message, jnp.concatenate(moments, axis=0), index)


def update_kernel(
    residual, image, first_message, message, neumann, basis, share, order,
    fresh, partial, scalars, *send,
):
    picked = get_message(message)
    rz, curve = picked[48:49], picked[49:50]
    step = rz / curve
    scalars[...] = jnp.concatenate([rz, curve, step, jnp.zeros((TILE - 3, LANES), F32)], axis=0)
    coarse = get_message(first_message) - step * picked
    for s in range(2):
        pieces = []
        for f in range(4):
            value = residual[s, rows(f), :] - step * image[s, rows(f), :]
            fresh[s, rows(f), :] = value
            pieces.append((share_of(share, s, f) * value).astype(BF16))
        local = dot(neumann[s], jnp.concatenate(pieces, axis=0))
        local = local + spread_basis(basis, s, coarse)
        for f in range(4):
            part = local[f * FACE : f * FACE + FACE]
            partial[s, rows(f), :] = share_of(share, s, f) * part
    put_faces(send, order, lambda s, f: partial[s, rows(f), :])


def last_kernel(
    partial, lower, upper, previous, following, inside, order, share, schur, residual, image,
    search, message,
):
    recv = (lower, upper, previous, following, inside)
    rz = jnp.zeros((1, LANES), F32)
    same = jnp.zeros((1, LANES), F32)
    cross = jnp.zeros((1, LANES), F32)
    for s in range(2):
        for f in range(4):
            value = partial[s, rows(f), :] + to_local(order[4 * s + f], partner(recv, s, f))
            search[s, rows(f), :] = value
            weighted = share_of(share, s, f) * residual[s, rows(f), :] * value
            rz = rz + jnp.sum(weighted, axis=0, keepdims=True)
        whole = search[s]
        rounded = whole.astype(BF16)
        product = dot(schur[s], rounded)
        twice = 2.0 * whole - rounded.astype(F32)
        same = same + jnp.sum(twice * product, axis=0, keepdims=True)
        cross = cross + jnp.sum(whole * image[s], axis=0, keepdims=True)
    tile = jnp.concatenate([rz, same, cross, jnp.zeros((TILE - 3, LANES), F32)], axis=0)
    for d in range(message.shape[0] // TILE):
        message[pl.ds(TILE * d, TILE), :] = tile


def sum_tiles(received):
    total = received[pl.ds(0, TILE), :]
    for d in range(1, received.shape[0] // TILE):
        total = total + received[pl.ds(TILE * d, TILE), :]
    return total


def sum_kernel(received, out):
    total = sum_tiles(received)
    for z in range(out.shape[0] // TILE):
        out[pl.ds(TILE * z, TILE), :] = total


def finish_kernel(received, scalars, direction, search, out):
    total = sum_tiles(received)
    rz, curve, step = scalars[0:1, :], scalars[1:2, :], scalars[2:3, :]
    rz_next, same, cross = total[0:1], total[1:2], total[2:3]
    beta = rz_next / rz
    curve_next = same + 2.0 * beta * cross + beta * beta * curve
    step_next = rz_next / curve_next
    along = step + step_next * beta
    for s in range(2):
        out[s] = along * direction[s] + step_next * search[s]


def body(loads, schur, neumann, basis, dof_order, primal_map, emitter_counts, coarse_inverse):
    n_grp = lax.axis_size("grp")
    n_sub = lax.axis_size("sub")
    n_z = n_sub // 2
    grp = lax.axis_index("grp")
    sub = lax.axis_index("sub")
    place = jnp.stack([grp, sub, jnp.int32(n_grp), jnp.int32(n_sub)]).astype(jnp.int32)
    vector = ((2, 4 * FACE, LANES), F32)
    tile = ((TILE, LANES), F32)
    owners = 2 * n_grp
    message_shape = ((owners * TILE, LANES), F32)

    plane = [
        [g * n_sub + 2 * z + c for g in range(n_grp) for c in range(2)] for z in range(n_z)
    ]
    column = [
        [g * n_sub + 2 * z + c for z in range(n_z)] for g in range(n_grp) for c in range(2)
    ]

    def to_owners(value):
        return lax.all_to_all(value, AXES, 0, 0, axis_index_groups=plane, tiled=True)

    def along_z(value):
        return lax.all_to_all(value, AXES, 0, 0, axis_index_groups=column, tiled=True)

    prim = primal_map.size
    index = jnp.pad(
        primal_map.reshape(1, prim).astype(F32), ((0, 0), (0, LANES - prim)), constant_values=-1.0
    )
    swap = [(i, i ^ 1) for i in range(n_sub)]
    other = lax.ppermute(coarse_inverse, "sub", swap)
    order, share, *send = call(
        prepare_kernel,
        [((8, FACE, FACE), BF16), tile] + HALO_SHAPES,
        place, emitter_counts, dof_order, loads,
        smem=(0, 1),
    )
    recv = exchange(send)
    high, low = call(
        coarse_split_kernel,
        [((2 * LANES, coarse_inverse.shape[1]), BF16)] * 2,
        place, coarse_inverse, other,
        smem=(0,),
    )

    def coarse_solve(message, first):
        received = to_owners(message)
        if first is None:
            first = received
        (gathered,) = pl.pallas_call(
            scatter_kernel,
            out_shape=[jax.ShapeDtypeStruct((n_z * GATHER, LANES), F32)],
            in_specs=[pl.BlockSpec(memory_space=pltpu.VMEM)],
            out_specs=[pl.BlockSpec(memory_space=pltpu.VMEM)],
            scratch_shapes=[
                pltpu.VMEM((2 * LANES, owners * LANES), BF16),
                pltpu.VMEM((LANES, owners * LANES), BF16),
            ],
            compiler_params=pltpu.CompilerParams(vmem_limit_bytes=VMEM_LIMIT),
        )(received)
        gathered = along_z(gathered)
        slab, scalars = call(coarse_kernel, [((n_z * TILE, LANES), F32), tile], gathered, high, low)
        coarse = along_z(slab)
        (picked,) = call(pick_kernel, [message_shape], coarse, first, scalars)
        return to_owners(picked), first

    residual, local, message = call(
        residual_kernel,
        [vector, vector, message_shape],
        loads, *recv, order, share, neumann, basis, index,
    )
    picked_first, maps = coarse_solve(message, None)
    partial, *send = call(
        search_kernel, [vector] + HALO_SHAPES, picked_first, local, basis, share, order
    )
    recv = exchange(send)
    direction, product, sums, *send = call(
        direction_kernel,
        [vector, vector, tile] + HALO_SHAPES,
        partial, *recv, order, share, schur, residual,
    )
    recv = exchange(send)
    image, message = call(
        image_kernel,
        [vector, message_shape],
        product, *recv, order, share, basis, index, sums,
    )
    picked, _ = coarse_solve(message, maps)
    fresh, partial, scalars, *send = call(
        update_kernel,
        [vector, vector, tile] + HALO_SHAPES,
        residual, image, picked_first, picked, neumann, basis, share, order,
    )
    recv = exchange(send)
    search, message = call(
        last_kernel,
        [vector, message_shape],
        partial, *recv, order, share, schur, fresh, product,
    )
    (sums,) = call(sum_kernel, [((n_z * TILE, LANES), F32)], to_owners(message))
    (out,) = call(finish_kernel, [vector], along_z(sums), scalars, direction, search)
    return out


def solution(mesh):
    in_specs = (
        P(AXES, None, None),
        P(AXES, None, None),
        P(AXES, None, None),
        P(AXES, None, None),
        P(AXES, None, None),
        P(AXES, None),
        P(),
        P("sub", None),
    )
    return jax.shard_map(
        body, mesh=mesh, in_specs=in_specs, out_specs=P(AXES, None, None), check_vma=False
    )
```

time: 1220 us -> 224 us (0.18)
  waiting for transfers between devices: 606 us -> 24.3 us
  local copies, waits for them, and re-layouts: 260 us -> 13.3 us
  blocking collectives: 234 us -> 118 us
  matrix products: 33.7 us -> 0 us
  other arithmetic: 24.1 us -> 0.76 us
  Pallas kernels: 0 us -> 20.5 us
  between operations: 13.9 us -> 0.3 us
    psum x2 -> x0, waiting for transfers between devices: 509 us -> none  [precondition(): gathered = lax.psum(partial_rhs, ('grp', 'sub'))]
    gather x17 -> x0, local copies, waits for them, and re-layouts: 239 us -> none  [the longest x10 125 us: assemble(): return values + jnp.take_along_axis(partners, inverse[:, :, None], axis=1)]
    psum x3 -> x0, blocking collectives: 234 us -> none  [the longest x2 156 us: precondition(): inner_value = lax.psum(local_inner(residual, search), ('grp', 'sub'))]
    all_to_all x0 -> x9, blocking collectives: none -> 118 us  [the longest x5 74.1 us: to_owners(): lax.all_to_all(value, AXES, 0, 0, axis_index_groups=plane, tiled=True)]
    all_gather x2 -> x0, waiting for transfers between devices: 67.2 us -> none  [precondition(): coarse = lax.all_gather(coarse_slab, 'sub', axis=0, tiled=True)]
    dot_general x12 -> x0, matrix products: 33.7 us -> none  [the longest x2 9.37 us: precondition(): jnp.einsum('sij,sjr->sir', neumann, rounded, preferred_element_type=jnp.f...]
    pallas_call x0 -> x16, Pallas kernels: none -> 20.5 us  [the longest x14 16.6 us: call(): pl.pallas_call(kernel, out_shape=[jax.ShapeDtypeStruct(s, d) for s, d in...]
    ppermute x20 -> x17, waiting for transfers between devices: 29.7 us -> 16.3 us  [the longest x4 16.3 us: exchange(): following = lax.ppermute(before, 'sub', sub_down)]
  transfers between devices with their start and end apart: 24 -> 18, of which waited for: 13 -> 5; matrix products, arithmetic and copies ran while one was open for 1% -> 0% of each run, Pallas kernels for 0% -> 3%
where the time goes in v1:
time: 224 us; the launch traced here: 223 us
  blocking collectives  118 us (53%)
  starting transfers between devices  46.2 us (21%)
  waiting for transfers between devices  24.3 us (11%)
  Pallas kernels  20.5 us (9%)
  local copies, waits for them, and re-layouts  13.3 us (6%)
    all_to_all x5, blocking collectives, to_owners(): lax.all_to_all(value, AXES, 0, 0, axis_index_groups=plane, tiled=True)  74.1 us
    all_to_all x4, blocking collectives, along_z(): lax.all_to_all(value, AXES, 0, 0, axis_index_groups=column, tiled=True)  43.6 us
    pallas_call x14, Pallas kernels, call(): pl.pallas_call(kernel, out_shape=[jax.ShapeDtypeStruct(s, d) for s, d in...  16.6 us
    ppermute x4, waiting for transfers between devices, exchange(): following = lax.ppermute(before, 'sub', sub_down)  16.3 us
    unnamed x32, local copies, waits for them, and re-layouts  13.2 us
    ppermute x4, starting transfers between devices, exchange(): previous = lax.ppermute(after, 'sub', sub_up)  11.2 us
    ppermute x4, starting transfers between devices, exchange(): lower = lax.ppermute(up, 'grp', grp_up)  10.5 us
    all_to_all x1, starting transfers between devices, along_z(): lax.all_to_all(value, AXES, 0, 0, axis_index_groups=column, tiled=True)  8.04 us
  transfers between devices with their start and end apart: 18, of which 5 were waited for; matrix products, arithmetic and copies ran while one was open for 0% of the time, Pallas kernels for 3%

profile of v1, /device:TPU:1, one launch (start us, length us, event | category | flops | bytes accessed | tf_op | source)
XLA Modules:
  0.0 223.1 jit_solution(17128726120306733380)
XLA Ops:
  0.0 3.2 %collective-permute-start.4 = (f32[128,2048]{1,0:T(8,128)}, f32[128,2048]{1,0:T(8,128)S(1)}, u32[]{:S(2)}, u32[]{:S(2)}) collective-permute-start(f32[128,2048]{1,0:T(8,128)} %own.1), channel_id=1, source_target_pairs={{0,1},{1,0},{2,3},{3,2},{4,5},{5,4},{6,7},{7,6},{8,9},{9,8},{10,11... | collective-permute-start | bytes 3145736 | tf_op jit(solution)/shard_map/ppermute | solution.py:426
  10.2 3.7 %collective-permute-start.2 = (f32[256,128]{1,0:T(8,128)S(1)}, f32[256,128]{1,0:T(8,128)S(1)}, u32[]{:S(2)}, u32[]{:S(2)}) collective-permute-start(f32[256,128]{1,0:T(8,128)S(1)} %get-tuple-element.49), channel_id=1, source_target_pairs={{0,1},{1,2},{2,3},{3,4},{4,5},{5,6},{6,7},{7,8},{8,9},{9,10},{10,1... | collective-permute-start | bytes 393224 | tf_op jit(solution)/shard_map/ppermute | solution.py:117
  16.6 3.6 %collective-permute-done.3.following = f32[256,128]{1,0:T(8,128)S(1)} collective-permute-done((f32[256,128]{1,0:T(8,128)S(1)}, f32[256,128]{1,0:T(8,128)S(1)}, u32[]{:S(2)}, u32[]{:S(2)}) %collective-permute-start.3) | collective-permute-done | bytes 131104 | tf_op jit(solution)/shard_map/ppermute | solution.py:118
  28.0 15.9 %all_to_all.110 = f32[32,8,128]{2,1,0:T(8,128)S(1)} all-to-all(f32[32,8,128]{2,1,0:T(8,128)S(1)} %bitcast.40), channel_id=1, replica_groups={{0,1,16,17,32,33,48,49,64,65,80,81,96,97,112,113,128,129,144,145,160,16..., dimensions={0} | all-to-all | bytes 262144 | tf_op jit(solution)/shard_map/all_to_all | solution.py:416
  43.9 2.3 %shard_map.84 = f32[576,128]{1,0:T(8,128)} custom-call(f32[256,128]{1,0:T(8,128)S(1)} %bitcast.22), custom_call_target="tpu_custom_call" | custom-call | tf_op jit(solution)/shard_map/pallas_call | solution.py:445
  46.3 8.0 %all-to-all-start.1 = ((f32[8,72,128]{2,1,0:T(8,128)}), f32[8,72,128]{2,1,0:T(8,128)}, u32[]{:S(2)}, u32[]{:S(2)}) async-start(f32[8,72,128]{2,1,0:T(8,128)} %bitcast.4), calls=%async_computation.1 | async-start | bytes 589824 | tf_op jit(solution)/shard_map/all_to_all | solution.py:419
  58.7 8.0 %all-to-all-done.1 = f32[8,72,128]{2,1,0:T(8,128)} async-done(((f32[8,72,128]{2,1,0:T(8,128)}), f32[8,72,128]{2,1,0:T(8,128)}, u32[]{:S(2)}, u32[]{:S(2)}) %all-to-all-start.1) | async-done | bytes 294944 | tf_op jit(solution)/shard_map/all_to_all | solution.py:419
  68.5 9.2 %all_to_all.111 = f32[8,8,128]{2,1,0:T(8,128)S(1)} all-to-all(f32[8,8,128]{2,1,0:T(8,128)S(1)} %bitcast.42), channel_id=1, replica_groups={{0,2,4,6,8,10,12,14},{1,3,5,7,9,11,13,15},{16,18,20,22,24,26,28,30},{17..., dimensions={0} | all-to-all | bytes 65536 | tf_op jit(solution)/shard_map/all_to_all | solution.py:419
  78.2 13.1 %all_to_all.112 = f32[32,8,128]{2,1,0:T(8,128)S(1)} all-to-all(f32[32,8,128]{2,1,0:T(8,128)S(1)} %bitcast.31), channel_id=1, replica_groups={{0,1,16,17,32,33,48,49,64,65,80,81,96,97,112,113,128,129,144,145,160,16..., dimensions={0} | all-to-all | bytes 262144 | tf_op jit(solution)/shard_map/all_to_all | solution.py:416
  93.3 2.3 %collective-permute-start.5 = (f32[2,256,128]{2,1,0:T(8,128)S(1)}, f32[2,256,128]{2,1,0:T(8,128)S(1)}, u32[]{:S(2)}, u32[]{:S(2)}) collective-permute-start(f32[2,256,128]{2,1,0:T(8,128)S(1)} %get-tuple-element.62), channel_id=1, source_target_pairs={{0,16},{16,32},{32,48},{48,64},{64,80},{80,96},{96,112},{112,128},... | collective-permute-start | bytes 786440 | tf_op jit(solution)/shard_map/ppermute | solution.py:115
  96.9 2.7 %collective-permute-start.7 = (f32[256,128]{1,0:T(8,128)S(1)}, f32[256,128]{1,0:T(8,128)S(1)}, u32[]{:S(2)}, u32[]{:S(2)}) collective-permute-start(f32[256,128]{1,0:T(8,128)S(1)} %get-tuple-element.64), channel_id=1, source_target_pairs={{0,1},{1,2},{2,3},{3,4},{4,5},{5,6},{6,7},{7,8},{8,9},{9,10},{10,1... | collective-permute-start | bytes 393224 | tf_op jit(solution)/shard_map/ppermute | solution.py:117
  101.5 4.3 %collective-permute-done.8.following = f32[256,128]{1,0:T(8,128)S(1)} collective-permute-done((f32[256,128]{1,0:T(8,128)S(1)}, f32[256,128]{1,0:T(8,128)S(1)}, u32[]{:S(2)}, u32[]{:S(2)}) %collective-permute-start.8) | collective-permute-done | bytes 131104 | tf_op jit(solution)/shard_map/ppermute | solution.py:118
  108.0 4.5 %collective-permute-start.9 = (f32[2,256,128]{2,1,0:T(8,128)S(1)}, f32[2,256,128]{2,1,0:T(8,128)S(1)}, u32[]{:S(2)}, u32[]{:S(2)}) collective-permute-start(f32[2,256,128]{2,1,0:T(8,128)S(1)} %get-tuple-element.68), channel_id=1, source_target_pairs={{0,16},{16,32},{32,48},{48,64},{64,80},{80,96},{96,112},{112,128},... | collective-permute-start | bytes 786440 | tf_op jit(solution)/shard_map/ppermute | solution.py:115
  115.9 2.3 %collective-permute-start.12 = (f32[256,128]{1,0:T(8,128)S(1)}, f32[256,128]{1,0:T(8,128)S(1)}, u32[]{:S(2)}, u32[]{:S(2)}) collective-permute-start(f32[256,128]{1,0:T(8,128)S(1)} %get-tuple-element.71), channel_id=1, source_target_pairs={{1,0},{2,1},{3,2},{4,3},{5,4},{6,5},{7,6},{8,7},{9,8},{10,9},{11,1... | collective-permute-start | bytes 393224 | tf_op jit(solution)/shard_map/ppermute | solution.py:118
  118.2 4.0 %collective-permute-done.12.following = f32[256,128]{1,0:T(8,128)S(1)} collective-permute-done((f32[256,128]{1,0:T(8,128)S(1)}, f32[256,128]{1,0:T(8,128)S(1)}, u32[]{:S(2)}, u32[]{:S(2)}) %collective-permute-start.12) | collective-permute-done | bytes 131104 | tf_op jit(solution)/shard_map/ppermute | solution.py:118
  123.1 16.5 %all_to_all.113 = f32[32,8,128]{2,1,0:T(8,128)S(1)} all-to-all(f32[32,8,128]{2,1,0:T(8,128)S(1)} %bitcast.39), channel_id=1, replica_groups={{0,1,16,17,32,33,48,49,64,65,80,81,96,97,112,113,128,129,144,145,160,16..., dimensions={0} | all-to-all | bytes 262144 | tf_op jit(solution)/shard_map/all_to_all | solution.py:416
  141.1 15.9 %all_to_all.114 = f32[8,72,128]{2,1,0:T(8,128)S(1)} all-to-all(f32[8,72,128]{2,1,0:T(8,128)S(1)} %bitcast.28), channel_id=1, replica_groups={{0,2,4,6,8,10,12,14},{1,3,5,7,9,11,13,15},{16,18,20,22,24,26,28,30},{17..., dimensions={0} | all-to-all | bytes 589824 | tf_op jit(solution)/shard_map/all_to_all | solution.py:419
  157.7 9.2 %all_to_all.115 = f32[8,8,128]{2,1,0:T(8,128)S(1)} all-to-all(f32[8,8,128]{2,1,0:T(8,128)S(1)} %bitcast.41), channel_id=1, replica_groups={{0,2,4,6,8,10,12,14},{1,3,5,7,9,11,13,15},{16,18,20,22,24,26,28,30},{17..., dimensions={0} | all-to-all | bytes 65536 | tf_op jit(solution)/shard_map/all_to_all | solution.py:419
  167.4 13.4 %all_to_all.116 = f32[32,8,128]{2,1,0:T(8,128)S(1)} all-to-all(f32[32,8,128]{2,1,0:T(8,128)S(1)} %bitcast.30), channel_id=1, replica_groups={{0,1,16,17,32,33,48,49,64,65,80,81,96,97,112,113,128,129,144,145,160,16..., dimensions={0} | all-to-all | bytes 262144 | tf_op jit(solution)/shard_map/all_to_all | solution.py:416
  183.0 2.3 %collective-permute-start.13 = (f32[2,256,128]{2,1,0:T(8,128)S(1)}, f32[2,256,128]{2,1,0:T(8,128)S(1)}, u32[]{:S(2)}, u32[]{:S(2)}) collective-permute-start(f32[2,256,128]{2,1,0:T(8,128)S(1)} %get-tuple-element.79), channel_id=1, source_target_pairs={{0,16},{16,32},{32,48},{48,64},{64,80},{80,96},{96,112},{112,128},... | collective-permute-start | bytes 786440 | tf_op jit(solution)/shard_map/ppermute | solution.py:115
  186.6 2.7 %collective-permute-start.15 = (f32[256,128]{1,0:T(8,128)S(1)}, f32[256,128]{1,0:T(8,128)S(1)}, u32[]{:S(2)}, u32[]{:S(2)}) collective-permute-start(f32[256,128]{1,0:T(8,128)S(1)} %get-tuple-element.81), channel_id=1, source_target_pairs={{0,1},{1,2},{2,3},{3,4},{4,5},{5,6},{6,7},{7,8},{8,9},{9,10},{10,1... | collective-permute-start | bytes 393224 | tf_op jit(solution)/shard_map/ppermute | solution.py:117
  191.2 4.3 %collective-permute-done.16.following = f32[256,128]{1,0:T(8,128)S(1)} collective-permute-done((f32[256,128]{1,0:T(8,128)S(1)}, f32[256,128]{1,0:T(8,128)S(1)}, u32[]{:S(2)}, u32[]{:S(2)}) %collective-permute-start.16) | collective-permute-done | bytes 131104 | tf_op jit(solution)/shard_map/ppermute | solution.py:118
  197.4 15.3 %all_to_all.117 = f32[32,8,128]{2,1,0:T(8,128)S(1)} all-to-all(f32[32,8,128]{2,1,0:T(8,128)S(1)} %bitcast.38), channel_id=1, replica_groups={{0,1,16,17,32,33,48,49,64,65,80,81,96,97,112,113,128,129,144,145,160,16..., dimensions={0} | all-to-all | bytes 262144 | tf_op jit(solution)/shard_map/all_to_all | solution.py:416
  212.7 9.2 %all_to_all.118 = f32[8,8,128]{2,1,0:T(8,128)S(1)} all-to-all(f32[8,8,128]{2,1,0:T(8,128)S(1)} %bitcast.37), channel_id=1, replica_groups={{0,2,4,6,8,10,12,14},{1,3,5,7,9,11,13,15},{16,18,20,22,24,26,28,30},{17..., dimensions={0} | all-to-all | bytes 65536 | tf_op jit(solution)/shard_map/all_to_all | solution.py:419
  (74 shorter events, 46.6 us)
Async XLA Ops:
  0.0 54.3 %collective-permute-start.4 = (f32[128,2048]{1,0:T(8,128)}, f32[128,2048]{1,0:T(8,128)S(1)}, u32[]{:S(2)}, u32[]{:S(2)}) collective-permute-start(f32[128,2048]{1,0:T(8,128)} %own.1), channel_id=1, source_target_pairs={{0,1},{1,0},{2,3},{3,2},{4,5},{5,4},{6,7},{7,6},{8,9},{9,8},{10,11... | collective-permute-start | bytes 3145736 | tf_op jit(solution)/shard_map/ppermute | solution.py:426
  7.5 12.7 %collective-permute-start = (f32[2,256,128]{2,1,0:T(8,128)}, f32[2,256,128]{2,1,0:T(8,128)S(1)}, u32[]{:S(2)}, u32[]{:S(2)}) collective-permute-start(f32[2,256,128]{2,1,0:T(8,128)} %get-tuple-element.47), channel_id=1, source_target_pairs={{0,16},{16,32},{32,48},{48,64},{64,80},{80,96},{96,112},{112,128},... | collective-permute-start | bytes 786440 | tf_op jit(solution)/shard_map/ppermute | solution.py:115
  8.9 11.3 %collective-permute-start.1 = (f32[2,256,128]{2,1,0:T(8,128)}, f32[2,256,128]{2,1,0:T(8,128)S(1)}, u32[]{:S(2)}, u32[]{:S(2)}) collective-permute-start(f32[2,256,128]{2,1,0:T(8,128)} %get-tuple-element.48), channel_id=1, source_target_pairs={{16,0},{32,16},{48,32},{64,48},{80,64},{96,80},{112,96},{128,112},... | collective-permute-start | bytes 786440 | tf_op jit(solution)/shard_map/ppermute | solution.py:116
  10.2 6.4 %collective-permute-start.2 = (f32[256,128]{1,0:T(8,128)S(1)}, f32[256,128]{1,0:T(8,128)S(1)}, u32[]{:S(2)}, u32[]{:S(2)}) collective-permute-start(f32[256,128]{1,0:T(8,128)S(1)} %get-tuple-element.49), channel_id=1, source_target_pairs={{0,1},{1,2},{2,3},{3,4},{4,5},{5,6},{6,7},{7,8},{8,9},{9,10},{10,1... | collective-permute-start | bytes 393224 | tf_op jit(solution)/shard_map/ppermute | solution.py:117
  13.9 6.3 %collective-permute-start.3 = (f32[256,128]{1,0:T(8,128)S(1)}, f32[256,128]{1,0:T(8,128)S(1)}, u32[]{:S(2)}, u32[]{:S(2)}) collective-permute-start(f32[256,128]{1,0:T(8,128)S(1)} %get-tuple-element.50), channel_id=1, source_target_pairs={{1,0},{2,1},{3,2},{4,3},{5,4},{6,5},{7,6},{8,7},{9,8},{10,9},{11,1... | collective-permute-start | bytes 393224 | tf_op jit(solution)/shard_map/ppermute | solution.py:118
  20.2 2.2 copy-start
  28.0 63.3 %copy-start.8 = (bf16[2,24,1024]{2,1,0:T(8,128)(2,1)S(1)}, bf16[2,24,1024]{2,1,0:T(8,128)(2,1)}, u32[]{:S(2)}) copy-start(bf16[2,24,1024]{2,1,0:T(8,128)(2,1)} %basis.7) | copy-start | bytes 294916
  46.3 20.5 %all-to-all-start.1 = ((f32[8,72,128]{2,1,0:T(8,128)}), f32[8,72,128]{2,1,0:T(8,128)}, u32[]{:S(2)}, u32[]{:S(2)}) async-start(f32[8,72,128]{2,1,0:T(8,128)} %bitcast.4), calls=%async_computation.1 | async-start | bytes 589824 | tf_op jit(solution)/shard_map/all_to_all | solution.py:419
  66.7 39.2 %copy-start.2 = (bf16[2,1024,1024]{2,1,0:T(8,128)(2,1)S(1)}, bf16[2,1024,1024]{2,1,0:T(8,128)(2,1)}, u32[]{:S(2)}) copy-start(bf16[2,1024,1024]{2,1,0:T(8,128)(2,1)} %schur.3) | copy-start | bytes 12582916
  66.7 39.2 %copy-start.4 = (f32[2,1024,128]{2,1,0:T(8,128)S(1)}, f32[2,1024,128]{2,1,0:T(8,128)}, u32[]{:S(2)}) copy-start(f32[2,1024,128]{2,1,0:T(8,128)} %copy-done.3) | copy-start | bytes 3145732
  91.3 1.2 copy-start.13
  93.3 12.6 %collective-permute-start.5 = (f32[2,256,128]{2,1,0:T(8,128)S(1)}, f32[2,256,128]{2,1,0:T(8,128)S(1)}, u32[]{:S(2)}, u32[]{:S(2)}) collective-permute-start(f32[2,256,128]{2,1,0:T(8,128)S(1)} %get-tuple-element.62), channel_id=1, source_target_pairs={{0,16},{16,32},{32,48},{48,64},{64,80},{80,96},{96,112},{112,128},... | collective-permute-start | bytes 786440 | tf_op jit(solution)/shard_map/ppermute | solution.py:115
  95.6 10.3 %collective-permute-start.6 = (f32[2,256,128]{2,1,0:T(8,128)S(1)}, f32[2,256,128]{2,1,0:T(8,128)S(1)}, u32[]{:S(2)}, u32[]{:S(2)}) collective-permute-start(f32[2,256,128]{2,1,0:T(8,128)S(1)} %get-tuple-element.63), channel_id=1, source_target_pairs={{16,0},{32,16},{48,32},{64,48},{80,64},{96,80},{112,96},{128,112},... | collective-permute-start | bytes 786440 | tf_op jit(solution)/shard_map/ppermute | solution.py:116
  96.9 4.7 %collective-permute-start.7 = (f32[256,128]{1,0:T(8,128)S(1)}, f32[256,128]{1,0:T(8,128)S(1)}, u32[]{:S(2)}, u32[]{:S(2)}) collective-permute-start(f32[256,128]{1,0:T(8,128)S(1)} %get-tuple-element.64), channel_id=1, source_target_pairs={{0,1},{1,2},{2,3},{3,4},{4,5},{5,6},{6,7},{7,8},{8,9},{9,10},{10,1... | collective-permute-start | bytes 393224 | tf_op jit(solution)/shard_map/ppermute | solution.py:117
  99.6 6.3 %collective-permute-start.8 = (f32[256,128]{1,0:T(8,128)S(1)}, f32[256,128]{1,0:T(8,128)S(1)}, u32[]{:S(2)}, u32[]{:S(2)}) collective-permute-start(f32[256,128]{1,0:T(8,128)S(1)} %get-tuple-element.65), channel_id=1, source_target_pairs={{1,0},{2,1},{3,2},{4,3},{5,4},{6,5},{7,6},{8,7},{9,8},{10,9},{11,1... | collective-permute-start | bytes 393224 | tf_op jit(solution)/shard_map/ppermute | solution.py:118
  108.0 72.8 %copy-start.1 = (bf16[2,1024,1024]{2,1,0:T(8,128)(2,1)S(1)}, bf16[2,1024,1024]{2,1,0:T(8,128)(2,1)}, u32[]{:S(2)}) copy-start(bf16[2,1024,1024]{2,1,0:T(8,128)(2,1)} %neumann.3) | copy-start | bytes 12582916
  108.0 14.2 %collective-permute-start.9 = (f32[2,256,128]{2,1,0:T(8,128)S(1)}, f32[2,256,128]{2,1,0:T(8,128)S(1)}, u32[]{:S(2)}, u32[]{:S(2)}) collective-permute-start(f32[2,256,128]{2,1,0:T(8,128)S(1)} %get-tuple-element.68), channel_id=1, source_target_pairs={{0,16},{16,32},{32,48},{48,64},{64,80},{80,96},{96,112},{112,128},... | collective-permute-start | bytes 786440 | tf_op jit(solution)/shard_map/ppermute | solution.py:115
  112.5 9.7 %collective-permute-start.10 = (f32[2,256,128]{2,1,0:T(8,128)S(1)}, f32[2,256,128]{2,1,0:T(8,128)S(1)}, u32[]{:S(2)}, u32[]{:S(2)}) collective-permute-start(f32[2,256,128]{2,1,0:T(8,128)S(1)} %get-tuple-element.69), channel_id=1, source_target_pairs={{16,0},{32,16},{48,32},{64,48},{80,64},{96,80},{112,96},{128,112},... | collective-permute-start | bytes 786440 | tf_op jit(solution)/shard_map/ppermute | solution.py:116
  113.8 4.3 %collective-permute-start.11 = (f32[256,128]{1,0:T(8,128)S(1)}, f32[256,128]{1,0:T(8,128)S(1)}, u32[]{:S(2)}, u32[]{:S(2)}) collective-permute-start(f32[256,128]{1,0:T(8,128)S(1)} %get-tuple-element.70), channel_id=1, source_target_pairs={{0,1},{1,2},{2,3},{3,4},{4,5},{5,6},{6,7},{7,8},{8,9},{9,10},{10,1... | collective-permute-start | bytes 393224 | tf_op jit(solution)/shard_map/ppermute | solution.py:117
  115.9 6.3 %collective-permute-start.12 = (f32[256,128]{1,0:T(8,128)S(1)}, f32[256,128]{1,0:T(8,128)S(1)}, u32[]{:S(2)}, u32[]{:S(2)}) collective-permute-start(f32[256,128]{1,0:T(8,128)S(1)} %get-tuple-element.71), channel_id=1, source_target_pairs={{1,0},{2,1},{3,2},{4,3},{5,4},{6,5},{7,6},{8,7},{9,8},{10,9},{11,1... | collective-permute-start | bytes 393224 | tf_op jit(solution)/shard_map/ppermute | solution.py:118
  183.0 12.6 %collective-permute-start.13 = (f32[2,256,128]{2,1,0:T(8,128)S(1)}, f32[2,256,128]{2,1,0:T(8,128)S(1)}, u32[]{:S(2)}, u32[]{:S(2)}) collective-permute-start(f32[2,256,128]{2,1,0:T(8,128)S(1)} %get-tuple-element.79), channel_id=1, source_target_pairs={{0,16},{16,32},{32,48},{48,64},{64,80},{80,96},{96,112},{112,128},... | collective-permute-start | bytes 786440 | tf_op jit(solution)/shard_map/ppermute | solution.py:115
  185.3 10.3 %collective-permute-start.14 = (f32[2,256,128]{2,1,0:T(8,128)S(1)}, f32[2,256,128]{2,1,0:T(8,128)S(1)}, u32[]{:S(2)}, u32[]{:S(2)}) collective-permute-start(f32[2,256,128]{2,1,0:T(8,128)S(1)} %get-tuple-element.80), channel_id=1, source_target_pairs={{16,0},{32,16},{48,32},{64,48},{80,64},{96,80},{112,96},{128,112},... | collective-permute-start | bytes 786440 | tf_op jit(solution)/shard_map/ppermute | solution.py:116
  186.6 4.7 %collective-permute-start.15 = (f32[256,128]{1,0:T(8,128)S(1)}, f32[256,128]{1,0:T(8,128)S(1)}, u32[]{:S(2)}, u32[]{:S(2)}) collective-permute-start(f32[256,128]{1,0:T(8,128)S(1)} %get-tuple-element.81), channel_id=1, source_target_pairs={{0,1},{1,2},{2,3},{3,4},{4,5},{5,6},{6,7},{7,8},{8,9},{9,10},{10,1... | collective-permute-start | bytes 393224 | tf_op jit(solution)/shard_map/ppermute | solution.py:117
  189.3 6.3 %collective-permute-start.16 = (f32[256,128]{1,0:T(8,128)S(1)}, f32[256,128]{1,0:T(8,128)S(1)}, u32[]{:S(2)}, u32[]{:S(2)}) collective-permute-start(f32[256,128]{1,0:T(8,128)S(1)} %get-tuple-element.82), channel_id=1, source_target_pairs={{1,0},{2,1},{3,2},{4,3},{5,4},{6,5},{7,6},{8,7},{9,8},{10,9},{11,1... | collective-permute-start | bytes 393224 | tf_op jit(solution)/shard_map/ppermute | solution.py:118
  (10 other events, 9.8 us)
